TPU v7x, 128 devices: a whole 4x4x4 slice. The times are simulated.
128 devices in a mesh: rows: 32 (over z, y, core), layer: 4 (over x).
Axes of the slice: x: 4, y: 4, z: 4, core: 2. Of those that a mesh axis runs over, the one named last changes fastest.
Arguments:
- train_grads: bfloat16 [32768, 8, 4096], P('rows', 'layer'), may hold values from -6 to 6
- query_grads: bfloat16 [256, 8, 4096], P('rows', 'layer'), may hold values from -0.059814453 to 0.059814453
- basis_out: float32 [8, 64, 64], P('layer'), may hold values from -0.75 to 0.75
- basis_in: float32 [8, 64, 64], P('layer'), may hold values from -0.75 to 0.75
- eigenvalues: float32 [8, 64, 64], P('layer'), may hold values from 0.02 to 2
- train_ids: int32 [32768], P('rows'), may hold values from 0 to 32767, each once
- query_ids: int32 [256], P('layer'), may hold values from 0 to 32767
Outputs:
- scores: float32 [32768, 256], P('rows', 'layer')
Inputs may be any that keep to these rules, and one draw needn't show every extreme that they name: `train_ids`: every id of the slab appears in exactly one train row.
All inputs are finite; a program needn't handle non-finite values.
Results may differ from a plain program's by a relative error of at most 0.0029.
Values may be sent and summed in bfloat16 or wider, within the bound.
A program may use at most 128 MiB of HBM per device.

v0:
```python
import jax
import jax.numpy as jnp
from jax import lax
from jax.sharding import PartitionSpec as P

DAMPING = 0.1


def precondition(query_grads, basis_out, basis_in, eigenvalues):
    count, layers, proj = query_grads.shape
    side = basis_out.shape[1]
    hp = lax.Precision.HIGHEST
    grads = query_grads.astype(jnp.float32).reshape(count, layers, side, side)
    rotated = jnp.einsum("lao,qlab->qlob", basis_out, grads, precision=hp)
    rotated = jnp.einsum("qlob,lbi->qloi", rotated, basis_in, precision=hp)
    scaled = rotated / (eigenvalues[None] + DAMPING)
    back = jnp.einsum("lao,qloi->qlai", basis_out, scaled, precision=hp)
    back = jnp.einsum("qlai,lbi->qlab", back, basis_in, precision=hp)
    return back.reshape(count, layers, proj).astype(jnp.bfloat16)


def body(train_grads, query_grads, basis_out, basis_in, eigenvalues, train_ids, query_ids):
    flat_train = train_grads.reshape(train_grads.shape[0], -1)
    mine = precondition(query_grads, basis_out, basis_in, eigenvalues)
    piece = lax.all_gather(mine, "rows", axis=0, tiled=True)
    flat_piece = piece.reshape(piece.shape[0], -1)
    terms = lax.dot_general(
        flat_train, flat_piece, (((1,), (1,)), ((), ())), preferred_element_type=jnp.float32
    )
    raw = lax.psum_scatter(terms, "layer", scatter_dimension=1, tiled=True)
    same = train_ids[:, None] == query_ids[None, :]
    return jnp.where(same, jnp.float32(0.0), raw)


def solution(mesh):
    placed = (
        P("rows", "layer", None),
        P("rows", "layer", None),
        P("layer", None, None),
        P("layer", None, None),
        P("layer", None, None),
        P("rows"),
        P("layer"),
    )
    return jax.shard_map(
        body, mesh=mesh, in_specs=placed, out_specs=P("rows", "layer"), check_vma=False
    )
```

profile of v0, /device:TPU:0, one launch (start us, length us, event | category | flops | bytes accessed | tf_op | source)
XLA Modules:
  0.0 122.7 jit_solution(16440486883411651674)
XLA Ops:
  6.5 0.0 copy-start
  6.5 0.0 all-gather.2.cloned.1.call-start
  6.5 0.9 broadcast_add_fusion
  7.4 1.1 reshape.11
  8.5 0.0 copy-done
  8.5 0.4 convolution_bitcast_fusion.1
  9.0 1.8 %fusion.5 = f32[8,2,64,64]{3,2,0,1:T(8,128)S(1)} fusion(f32[8,2,64,64]{2,3,0,1:T(8,128)S(1)} %convolution_bitcast_fusion.1, f32[2,64,64]{2,1,0:T(8,128)S(1)} %broadcast_add_fusion, f32[2,64,64]{2,1,0:T(8,128)} %param.10), kind=kOutput, calls=%fused_computation.6 | convolution fusion | flops 50397184 | bytes 589824 | tf_op jit(solution)/shard_map/qlob,lbi->qloi/dot_general | solution.py:15
  10.8 0.6 convolution_bitcast_fusion
  11.4 1.4 %fusion.6 = bf16[8,2,64,64]{3,2,0,1:T(8,128)(2,1)S(1)} fusion(f32[8,2,64,64]{3,2,0,1:T(8,128)S(1)} %convolution_bitcast_fusion, f32[2,64,64]{2,1,0:T(8,128)} %param.10), kind=kOutput, calls=%fused_computation.8 | convolution fusion | flops 50397184 | bytes 425984 | tf_op jit(solution)/shard_map/qlai,lbi->qlab/dot_general | solution.py:18
  12.9 0.9 convert_element_type.12
  13.8 0.0 all-gather.2.cloned.1.call-update
  13.8 0.0 copy-start.1
  13.8 0.0 copy-start.2
  13.8 0.2 reduce-scatter.2.cloned.1.call-start
  14.1 48.8 %all-gather.2.cloned.1.call-done = bf16[256,2,4096]{2,0,1:T(8,128)(2,1)} async-done(((bf16[8,2,4096]{2,0,1:T(8,128)(2,1)}), bf16[256,2,4096]{2,0,1:T(8,128)(2,1)}) %all-gather.2.cloned.1.call-update) | async-done | bytes 4194320 | tf_op jit(solution)/shard_map/all_gather | solution.py:25
  62.9 28.3 %fusion.2 = f32[1024,256]{0,1:T(8,128)} fusion(bf16[256,2,4096]{2,0,1:T(8,128)(2,1)} %all-gather.2.cloned.1.call-done, bf16[1024,2,4096]{2,1,0:T(2,128)(2,1)} %param.7), kind=kOutput, calls=%fused_computation.2 | convolution fusion | flops 4294967296 | bytes 22020096 | tf_op jit(solution)/shard_map/dot_general | solution.py:27
  91.2 0.0 reduce-scatter.2.cloned.1.call-update
  91.2 22.9 %reduce-scatter.2.cloned.1.call-done = f32[1024,64]{0,1:T(8,128)} async-done(((f32[1024,256]{0,1:T(8,128)}), f32[1024,64]{0,1:T(8,128)}) %reduce-scatter.2.cloned.1.call-update) | async-done | bytes 262160 | tf_op jit(solution)/shard_map/reduce_scatter | solution.py:30
  114.1 0.0 copy-done.1
  114.1 0.0 copy-done.2
  114.1 1.7 %compare_select_fusion = f32[1024,64]{0,1:T(8,128)} fusion(f32[1024,64]{0,1:T(8,128)} %reduce-scatter.2.cloned.1.call-done, s32[1024]{0:T(1024)S(1)} %copy-done.1, s32[64]{0:T(128)S(1)} %copy-done.2), kind=kLoop, calls=%fused_computation.10 | loop fusion | flops 131072 | bytes 528640 | tf_op jit(solution)/shard_map/jit(_where)/select_n | solution.py:32
Async XLA Ops:
  6.5 2.0 %copy-start = (f32[2,64,64]{2,1,0:T(8,128)S(1)}, f32[2,64,64]{2,1,0:T(8,128)}, u32[]{:S(2)}) copy-start(f32[2,64,64]{2,1,0:T(8,128)} %param.9) | copy-start | bytes 98308
  6.5 56.3 %all-gather.2.cloned.1.call-start = ((), (), s32[]{:S(2)}) async-start(), calls=%async_computation.1 | async-start | bytes 4325376 | tf_op jit(solution)/shard_map/all_gather | solution.py:25
  13.8 100.3 %copy-start.1 = (s32[1024]{0:T(1024)S(1)}, s32[1024]{0:T(1024)}, u32[]{:S(2)}) copy-start(s32[1024]{0:T(1024)} %param.12) | copy-start | bytes 12292
  13.8 100.3 %copy-start.2 = (s32[64]{0:T(128)S(1)}, s32[64]{0:T(128)}, u32[]{:S(2)}) copy-start(s32[64]{0:T(128)} %param.13) | copy-start | bytes 772
  13.8 100.2 %reduce-scatter.2.cloned.1.call-start = ((), (), s32[]{:S(2)}) async-start(), calls=%async_computation.2 | async-start | bytes 1310720 | tf_op jit(solution)/shard_map/reduce_scatter | solution.py:30
Sparse Core Ops, SparseCore 0:
  13.9 48.8 all-gather.1
  91.3 22.7 reduce-scatter.1
where the time goes:
time: 123 us
  waiting for transfers between devices  71.7 us (58%)
  matrix products  32.6 us (27%)
  between operations  13.5 us (11%)
  other arithmetic  2.62 us (2%)
  local copies, waits for them, and re-layouts  2.06 us (2%)
    all_gather x1, waiting for transfers between devices, body(): piece = lax.all_gather(mine, 'rows', axis=0, tiled=True)  48.8 us
    dot_general x1, matrix products, body(): lax.dot_general(flat_train, flat_piece, (((1,), (1,)), ((), ())), preferr...  28.3 us
    reduce_scatter x1, waiting for transfers between devices, body(): raw = lax.psum_scatter(terms, 'layer', scatter_dimension=1, tiled=True)  22.9 us
  transfers between devices with their start and end apart: 2, of which 2 were waited for; matrix products, arithmetic and copies ran while one was open for 0% of the time, Pallas kernels for 0%

commit v1 on v0

v1 whole, which is shorter than its diff:
```python
import functools

import jax
import jax.numpy as jnp
from jax import lax
from jax.experimental import pallas as pl
from jax.experimental.pallas import tpu as pltpu
from jax.sharding import PartitionSpec as P

DAMPING = 0.1
MESH = pl.DeviceIdType.MESH
PAIRS = 4
WIDE = 4096 // PAIRS
HALF = WIDE // 2
CB = WIDE // 128
NT = (((1,), (1,)), ((), ()))
NN = (((1,), (0,)), ((), ()))
F32, BF16 = jnp.float32, jnp.bfloat16

OPS = (
    "Z1p", "Z1m", "Z2", "Z3A", "Z3B", "Z4B",
    "Y1A", "Y1B", "Y2B", "Y3Ap", "Y3Am", "Y4A", "Y3Bp", "Y3Bm", "Y4B",
    "DA", "DB",
)
OP = {name: place for place, name in enumerate(OPS)}


def split(value):
    high = value.astype(BF16)
    return high, (value - high.astype(F32)).astype(BF16)


def dot(a, b, dims=NN):
    return lax.dot_general(a, b, dims, preferred_element_type=F32)


def dot3(a, b, dims=NN):
    ah, al = split(a)
    bh, bl = split(b)
    return dot(ah, bh, dims) + (dot(al, bh, dims) + dot(ah, bl, dims))


def diagonal(block):
    wide = jnp.concatenate([block] * 4, axis=1)
    tall = jnp.concatenate([wide] * 4, axis=0)
    row = lax.broadcasted_iota(jnp.int32, (256, 256), 0) // 64
    col = lax.broadcasted_iota(jnp.int32, (256, 256), 1) // 64
    return jnp.where(row == col, tall, 0.0)


def kernel(
    train, query, basis_out, basis_in, eigenvalues, tids, qids, out,
    x, raw, flat, shaped, g, zacc, part, sb1, rb1, sb2, rb2,
    train_sem, raw_sem, send, recv, rs_send, rs_recv,
):
    rows, lay = lax.axis_index("rows"), lax.axis_index("layer")
    core = lax.rem(rows, 2)
    y = lax.rem(rows // 2, 4)
    z = rows // 8

    def at(dz, dy):
        return (lax.rem(z + dz + 4, 4) * 8 + lax.rem(y + dy + 4, 4) * 2 + core, lay)

    zp, zm, yp, ym = at(1, 0), at(-1, 0), at(0, 1), at(0, -1)
    sib = (rows + 1 - 2 * core, lay)
    lay1 = lay + 1 - 2 * lax.rem(lay, 2)
    x1, x3 = (rows, lay1), (rows, 3 - lay)
    lay2 = 3 - lay1
    iz_p, iz_m = lax.rem(z + 1, 4), lax.rem(z + 3, 4)

    barrier = pltpu.get_barrier_semaphore()
    for other in (sib, zp, zm, yp, ym, x1, x3):
        pl.semaphore_signal(barrier, inc=1, device_id=other, device_id_type=MESH)

    own_raw = pltpu.make_async_copy(query, raw.at[core], raw_sem.at[2])
    own_raw.start()
    def train_copy(cb):
        return pltpu.make_async_copy(train.at[:, cb], x.at[cb], train_sem.at[cb])

    for cb in range(32):
        train_copy(cb).start()

    bo, bi = basis_out[core], basis_in[core]
    left = diagonal(bo)
    left_t = diagonal(bo.T)
    right = diagonal(bi)
    scale = eigenvalues[core] + DAMPING
    scale = jnp.concatenate([jnp.concatenate([scale] * 4, axis=1)] * 4, axis=0)

    pl.semaphore_wait(barrier, 7)
    swap = pltpu.make_async_remote_copy(
        src_ref=query, dst_ref=raw.at[core], send_sem=raw_sem.at[0], recv_sem=raw_sem.at[1],
        device_id=sib, device_id_type=MESH,
    )
    swap.start()
    own_raw.wait()
    swap.wait()

    flat[...] = raw.reshape(1024, 128)[...].astype(F32)
    low = lax.broadcasted_iota(jnp.int32, (32, 128), 1) < 64
    for grp in range(4):
        for jh in range(2):
            q0 = 4 * grp + 2 * jh
            n0 = flat[pl.ds(q0 * 64 + core, 32, 2), :]
            n1 = flat[pl.ds(q0 * 64 + 64 + core, 32, 2), :]
            shaped[jh, pl.ds(grp * 64, 32, 2), :] = jnp.where(low, n0, pltpu.roll(n1, 64, 1))
            shaped[jh, pl.ds(grp * 64 + 1, 32, 2), :] = jnp.where(low, pltpu.roll(n0, 64, 1), n1)
    grads = jnp.concatenate([shaped[0], shaped[1]], axis=1).astype(BF16)
    lh, ll = split(left_t)
    rotated = dot3(dot(lh, grads) + dot(ll, grads), right)
    back = dot3(dot3(left, rotated / scale), right, NT)
    shaped[0] = back[:, :128]
    shaped[1] = back[:, 128:]
    for grp in range(4):
        for jh in range(2):
            q0 = 4 * grp + 2 * jh
            even = shaped[jh, pl.ds(grp * 64, 32, 2), :]
            odd = shaped[jh, pl.ds(grp * 64 + 1, 32, 2), :]
            flat[pl.ds(q0 * 32, 32), :] = jnp.where(low, even, pltpu.roll(odd, 64, 1))
            flat[pl.ds(q0 * 32 + 32, 32), :] = jnp.where(low, pltpu.roll(even, 64, 1), odd)
    for cb in range(32):
        g[core, 0, z, :, cb * 128:(cb + 1) * 128] = flat[pl.ds(cb, 16, 32), :].astype(BF16)

    every = slice(None)
    near, far = pl.ds(0, 2), pl.ds(2, 2)

    def copies(p):
        zc = pl.ds(pl.multiple_of(p * WIDE, WIDE), HALF)
        yc = pl.ds(pl.multiple_of(p * WIDE + HALF, HALF), HALF)
        both = pl.ds(pl.multiple_of(p * WIDE, WIDE), WIDE)
        odd = lax.rem(p, 2)
        way = 1 - 2 * odd
        zw, yw = at(way, 0), at(0, -way)
        behind = lax.rem(z - way + 4, 4)
        hop = 1 + 2 * odd
        table = {
            "Z1p": ((0, z, zc), (0, z, zc), zp),
            "Z1m": ((0, z, zc), (0, z, zc), zm),
            "Z2": ((0, behind, zc), (0, behind, zc), zw),
            "Z3A": ((0, every, zc), (1, every, zc), ym),
            "Z3B": ((0, every, zc), (3, every, zc), yp),
            "Z4B": ((hop, every, zc), (2, every, zc), yw),
            "Y1A": ((0, z, yc), (1, z, yc), ym),
            "Y1B": ((0, z, yc), (3, z, yc), yp),
            "Y2B": ((hop, z, yc), (2, z, yc), yw),
            "Y3Ap": ((near, z, yc), (near, z, yc), zp),
            "Y3Am": ((near, z, yc), (near, z, yc), zm),
            "Y4A": ((near, behind, yc), (near, behind, yc), zw),
            "Y3Bp": ((far, z, yc), (far, z, yc), zp),
            "Y3Bm": ((far, z, yc), (far, z, yc), zm),
            "Y4B": ((far, behind, yc), (far, behind, yc), zw),
            "DA": ((near, every, both), (near, every, both), sib),
            "DB": ((far, every, both), (far, every, both), sib),
        }

        def make(name):
            (d0, z0, c0), (d1, z1, c1), device = table[name]
            return pltpu.make_async_remote_copy(
                src_ref=g.at[core, d0, z0, every, c0], dst_ref=g.at[core, d1, z1, every, c1],
                send_sem=send.at[OP[name], p], recv_sem=recv.at[OP[name], p],
                device_id=device, device_id_type=MESH,
            )

        return make

    def go(p, *names):
        make = copies(p)
        for name in names:
            make(name).start()

    def got(p, *names):
        make = copies(p)
        for name in names:
            make(name).wait_recv()

    def stage1(p):
        go(p, "Z1p", "Z1m", "Y1A", "Y1B")

    def stage2(p):
        got(p, "Z1p", "Z1m")
        go(p, "Z2")
        got(p, "Y1A")
        go(p, "Y3Ap", "Y3Am")

    def stage3(p):
        got(p, "Z2")
        go(p, "Z3A", "Z3B")
        got(p, "Y3Ap", "Y3Am")
        go(p, "Y4A")
        got(p, "Y1B")
        go(p, "Y2B")

    def stage4(p):
        got(p, "Z3A", "Y4A")
        go(p, "DA")
        got(p, "Z3B")
        go(p, "Z4B")
        got(p, "Y2B")
        go(p, "Y3Bp", "Y3Bm")

    def stage5(p):
        got(p, "Y3Bp", "Y3Bm")
        go(p, "Y4B")

    def stage6(p):
        got(p, "Z4B", "Y4B")
        go(p, "DB")

    xr = x.reshape(32, 2048, 128)
    first = lax.rem(lax.broadcasted_iota(jnp.int32, (2048, 128), 0), 2) == 0

    def product(side, p):
        got(p, "DA" if side == 0 else "DB")
        if side == 0:
            for j in range(CB):
                train_copy(p * CB + j).wait()
        cols = pl.ds(pl.multiple_of(p * WIDE, WIDE), WIDE)
        weights = jnp.concatenate(
            [
                g[layer, 2 * side + dy, iz, :, cols]
                for layer in range(2)
                for iz in range(4)
                for dy in range(2)
            ],
            axis=0,
        )
        lhs = jnp.concatenate([xr[p * CB + j] for j in range(CB)], axis=1)
        both = dot(lhs, weights, NT)
        zacc[...] += jnp.where(first, both[:, :128], both[:, 128:])

    def reduce_copy(side, step, h):
        src, dst = ((sb1, rb1), (sb2, rb2))[step]
        return pltpu.make_async_remote_copy(
            src_ref=src.at[side, h], dst_ref=dst.at[side, h],
            send_sem=rs_send.at[side, step, h], recv_sem=rs_recv.at[side, step, h],
            device_id=(x1, x3)[step ^ h], device_id_type=MESH,
        )

    mates = (lay1, 3 - lay)

    def target(side, which, h):
        return part[side, pl.ds(pl.multiple_of(which * 32, 32), 32), h * 512:(h + 1) * 512]

    def scatter1(side):
        both = zacc[pl.ds(0, 1024, 2), :] + zacc[pl.ds(1, 1024, 2), :]
        part[side] = both.T
        for h in range(2):
            sb1[side, h, 0] = target(side, mates[h], h).astype(BF16)
            sb1[side, h, 1] = target(side, lay2, h).astype(BF16)
            reduce_copy(side, 0, h).start()

    def scatter2(side):
        for h in range(2):
            reduce_copy(side, 0, h).wait_recv()
            sb2[side, h] = (target(side, mates[1 - h], h) + rb1[side, h, 1].astype(F32)).astype(BF16)
            reduce_copy(side, 1, h).start()

    def finish(side):
        for h in range(2):
            reduce_copy(side, 1, h).wait_recv()
            cols = slice(h * 512, (h + 1) * 512)
            total = target(side, lay, h) + rb1[side, h, 0].astype(F32) + rb2[side, h].astype(F32)
            for dy in range(2):
                place = pl.ds(pl.multiple_of(lax.rem(y + 2 * side + dy, 4) * 16, 16), 16)
                same = qids[place, :] == tids[:, cols]
                out[place, cols] = jnp.where(same, 0.0, total[dy * 16:(dy + 1) * 16])
        for step in range(2):
            for h in range(2):
                reduce_copy(side, step, h).wait_send()

    def when(p, what):
        pl.when(jnp.logical_and(p >= 0, p < PAIRS))(functools.partial(what, p))

    zacc[...] = jnp.zeros_like(zacc)
    for p in range(PAIRS):
        stage1(p)

    @pl.loop(0, PAIRS + 4)
    def _(s):
        when(s, stage2)
        when(s - 1, stage3)
        when(s - 2, stage4)
        when(s - 3, functools.partial(product, 0))
        when(s - 3, stage5)
        when(s - 4, stage6)

    scatter1(0)
    zacc[...] = jnp.zeros_like(zacc)

    @pl.loop(0, PAIRS)
    def _(p):
        product(1, p)
        pl.when(p == 1)(functools.partial(scatter2, 0))
        pl.when(p == 2)(functools.partial(finish, 0))

    scatter1(1)
    scatter2(1)
    finish(1)

    @pl.loop(0, PAIRS)
    def _(p):
        make = copies(p)
        for name in OPS:
            make(name).wait_send()


def body(train_grads, query_grads, basis_out, basis_in, eigenvalues, train_ids, query_ids):
    train = train_grads.reshape(1024, 2, 32, 128).transpose(0, 2, 1, 3)
    query = query_grads.reshape(8, 2, 32, 128).transpose(0, 2, 1, 3)
    vmem = pl.BlockSpec(memory_space=pltpu.VMEM)
    hbm = pl.BlockSpec(memory_space=pl.ANY)
    dma = pltpu.SemaphoreType.DMA
    scores = pl.pallas_call(
        kernel,
        out_shape=jax.ShapeDtypeStruct((64, 1024), F32),
        in_specs=[hbm, hbm, vmem, vmem, vmem, vmem, vmem],
        out_specs=vmem,
        scratch_shapes=[
            pltpu.VMEM((32, 1024, 2, 128), BF16),
            pltpu.VMEM((2, 8, 32, 2, 128), BF16),
            pltpu.VMEM((1024, 128), F32),
            pltpu.VMEM((2, 256, 128), F32),
            pltpu.VMEM((2, 4, 4, 16, 4096), BF16),
            pltpu.VMEM((2048, 128), F32),
            pltpu.VMEM((2, 128, 1024), F32),
            pltpu.VMEM((2, 2, 2, 32, 512), BF16),
            pltpu.VMEM((2, 2, 2, 32, 512), BF16),
            pltpu.VMEM((2, 2, 32, 512), BF16),
            pltpu.VMEM((2, 2, 32, 512), BF16),
            dma((32,)),
            dma((3,)),
            dma((len(OPS), PAIRS)),
            dma((len(OPS), PAIRS)),
            dma((2, 2, 2)),
            dma((2, 2, 2)),
        ],
        compiler_params=pltpu.CompilerParams(
            collective_id=0, has_side_effects=True, vmem_limit_bytes=56 * 2**20
        ),
    )(
        train, query, basis_out, basis_in, eigenvalues,
        train_ids.reshape(1, -1), query_ids.reshape(-1, 1),
    )
    return scores.T


def solution(mesh):
    placed = (
        P("rows", "layer", None),
        P("rows", "layer", None),
        P("layer", None, None),
        P("layer", None, None),
        P("layer", None, None),
        P("rows"),
        P("layer"),
    )
    return jax.shard_map(
        body, mesh=mesh, in_specs=placed, out_specs=P("rows", "layer"), check_vma=False
    )
```

time: 123 us -> 61.7 us (0.50)
  waiting for transfers between devices: 71.7 us -> 0 us
  Pallas kernels: 0 us -> 58.5 us
  matrix products: 32.6 us -> 0 us
  between operations: 13.5 us -> 0.01 us
  other arithmetic: 2.62 us -> 0 us
    pallas_call x0 -> x1, Pallas kernels: none -> 58.5 us  [body(): pl.pallas_call(kernel, out_shape=jax.ShapeDtypeStruct((64, 1024), F32), i...]
    all_gather x1 -> x0, waiting for transfers between devices: 48.8 us -> none  [body(): piece = lax.all_gather(mine, 'rows', axis=0, tiled=True)]
    dot_general x5 -> x0, matrix products: 32.6 us -> none  [the longest x1 28.3 us: body(): lax.dot_general(flat_train, flat_piece, (((1,), (1,)), ((), ())), preferr...]
    reduce_scatter x1 -> x0, waiting for transfers between devices: 22.9 us -> none  [body(): raw = lax.psum_scatter(terms, 'layer', scatter_dimension=1, tiled=True)]
    select_n x1 -> x0, other arithmetic: 1.74 us -> none  [body(): return jnp.where(same, jnp.float32(0.0), raw)]
    unnamed x6 -> x1, local copies, waits for them, and re-layouts: 0.02 us -> 1.67 us
  transfers between devices with their start and end apart: 2 -> 0, of which waited for: 2 -> 0; matrix products, arithmetic and copies ran while one was open for 0% -> 0% of each run, Pallas kernels for 0% -> 0%
where the time goes in v1:
time: 61.7 us; the launch traced here: 61.5 us
  Pallas kernels  58.5 us (95%)
  local copies, waits for them, and re-layouts  3.03 us (5%)
    pallas_call x1, Pallas kernels, body(): pl.pallas_call(kernel, out_shape=jax.ShapeDtypeStruct((64, 1024), F32), i...  58.5 us
    unnamed x1, local copies, waits for them, and re-layouts  1.67 us
    reshape x1, local copies, waits for them, and re-layouts, body(): query_ids.reshape(-1, 1)  1.36 us

profile of v1, /device:TPU:0, one launch (start us, length us, event | category | flops | bytes accessed | tf_op | source)
XLA Modules:
  0.0 61.5 jit_solution(16839766530895403226)
XLA Ops:
  0.0 1.4 %copy.8.qids = s32[64,1]{1,0:T(8,128)} copy(s32[64,1]{0,1:T(1,128)} %bitcast.13) | data formatting | bytes 512 | tf_op jit(solution)/shard_map/reshape | solution.py:342
  1.4 58.5 %shard_map.73 = f32[64,1024]{1,0:T(8,128)} custom-call(bf16[1024,32,2,128]{3,2,1,0:T(2,128)(2,1)} %bitcast.9, bf16[8,32,2,128]{3,2,1,0:T(2,128)(2,1)} %bitcast.11, f32[2,64,64]{2,1,0:T(8,128)} %basis_out.1, f32[2,64,64]{2,1,0:T(8,128)} %basis_in.1, f32[2,64,64]{2,1,0:T(8,128)} %eigenvalues.1, s32[1,1024]{1,0:T(1,128)} %bitcast.12, s32[64,1]{1,0:T(8,128)} %copy.8.qids), custom_call_target="tpu_custom_call" | custom-call | tf_op jit(solution)/shard_map/pallas_call | solution.py:313
  59.9 1.7 %copy.10 = f32[1024,64]{0,1:T(8,128)} copy(f32[1024,64]{0,1:T(8,128)} %bitcast.10) | data formatting | bytes 524288

commit v2 on v0

v2 whole, which is shorter than its diff:
```python
import functools

import jax
import jax.numpy as jnp
from jax import lax
from jax.experimental import pallas as pl
from jax.experimental.pallas import tpu as pltpu
from jax.sharding import PartitionSpec as P

DAMPING = 0.1
MESH = pl.DeviceIdType.MESH
PARTS = 8
WIDE = 4096 // PARTS
CB = WIDE // 128
ROWS = 512
NT = (((1,), (1,)), ((), ()))
NN = (((1,), (0,)), ((), ()))
F32, BF16 = jnp.float32, jnp.bfloat16

OPS = ("S1p", "S1m", "S1d", "S2p", "S2m", "S3", "D0", "Dp", "Dm", "D2")
OP = {name: place for place, name in enumerate(OPS)}


def split(value):
    high = value.astype(BF16)
    return high, (value - high.astype(F32)).astype(BF16)


def dot(a, b, dims=NN):
    return lax.dot_general(a, b, dims, preferred_element_type=F32)


def dot3(a, b, dims=NN):
    ah, al = split(a)
    bh, bl = split(b)
    return dot(ah, bh, dims) + (dot(al, bh, dims) + dot(ah, bl, dims))


def square(grid):
    return jnp.concatenate([jnp.concatenate(line, axis=1) for line in grid], axis=0)


def diagonal(blocks):
    row = lax.broadcasted_iota(jnp.int32, (256, 256), 0) // 64
    col = lax.broadcasted_iota(jnp.int32, (256, 256), 1) // 64
    return jnp.where(row == col, square([[block] * 4 for block in blocks]), 0.0)


def kernel(
    train, query, basis_out, basis_in, eigenvalues, tids, qids, out,
    x, flat, shaped, whole, outbox, g, zacc, part, sb1, rb1, sb2, rb2,
    train_sem, swap_sem, send, recv, rs_send, rs_recv,
):
    rows, lay = lax.axis_index("rows"), lax.axis_index("layer")
    core = lax.rem(rows, 2)
    y = lax.rem(rows // 2, 4)
    z = rows // 8

    def at(dz, dy):
        return (lax.rem(z + dz + 4, 4) * 8 + lax.rem(y + dy + 4, 4) * 2 + core, lay)

    def first_axis(k):
        return at(k * (1 - core), k * core)

    def second_axis(k):
        return at(k * core, k * (1 - core))

    a = jnp.where(core == 0, z, y)
    b = jnp.where(core == 0, y, z)
    sib = (rows + 1 - 2 * core, lay)
    lay1 = lay + 1 - 2 * lax.rem(lay, 2)
    x1, x3 = (rows, lay1), (rows, 3 - lay)
    lay2 = 3 - lay1

    barrier = pltpu.get_barrier_semaphore()
    for other in (sib, at(1, 0), at(-1, 0), at(0, 1), at(0, -1), first_axis(2), x1, x3):
        pl.semaphore_signal(barrier, inc=1, device_id=other, device_id_type=MESH)

    def train_copy(cb):
        return pltpu.make_async_copy(train.at[:, cb], x.at[cb], train_sem.at[cb])

    for cb in range(32):
        train_copy(cb).start()

    flat[...] = query.reshape(512, 128)[...].astype(F32)
    low = lax.broadcasted_iota(jnp.int32, (32, 128), 1) < 64
    for layer in range(2):
        for grp in range(2):
            for jh in range(2):
                q0 = 4 * grp + 2 * jh
                n0 = flat[pl.ds(q0 * 64 + layer, 32, 2), :]
                n1 = flat[pl.ds(q0 * 64 + 64 + layer, 32, 2), :]
                shaped[layer, jh, pl.ds(grp * 64, 32, 2), :] = jnp.where(low, n0, pltpu.roll(n1, 64, 1))
                shaped[layer, jh, pl.ds(grp * 64 + 1, 32, 2), :] = jnp.where(low, pltpu.roll(n0, 64, 1), n1)
    grads = jnp.concatenate(
        [jnp.concatenate([shaped[layer, 0], shaped[layer, 1]], axis=1) for layer in range(2)], axis=0
    ).astype(BF16)
    bo = (basis_out[0], basis_out[1])
    left = diagonal((bo[0], bo[0], bo[1], bo[1]))
    left_t = diagonal((bo[0].T, bo[0].T, bo[1].T, bo[1].T))
    right = [diagonal((basis_in[layer],) * 4) for layer in range(2)]
    scale = square([[eigenvalues[layer] + DAMPING] * 4 for layer in (0, 0, 1, 1)])

    def by_right(value, dims):
        return jnp.concatenate(
            [dot3(value[layer * 128:(layer + 1) * 128], right[layer], dims) for layer in range(2)], axis=0
        )

    lh, ll = split(left_t)
    rotated = by_right(dot(lh, grads) + dot(ll, grads), NN)
    back = by_right(dot3(left, rotated / scale), NT)
    for layer in range(2):
        for jh in range(2):
            shaped[layer, jh] = back[layer * 128:(layer + 1) * 128, jh * 128:(jh + 1) * 128]

    def unshape(layer, place, start):
        for grp in range(2):
            for jh in range(2):
                q0 = 4 * grp + 2 * jh
                even = shaped[layer, jh, pl.ds(grp * 64, 32, 2), :]
                odd = shaped[layer, jh, pl.ds(grp * 64 + 1, 32, 2), :]
                first = pl.multiple_of(start + q0 * 32, 32)
                place[pl.ds(first, 32), :] = jnp.where(low, even, pltpu.roll(odd, 64, 1))
                place[pl.ds(first + 32, 32), :] = jnp.where(low, pltpu.roll(even, 64, 1), odd)

    unshape(1 - core, outbox, 0)
    unshape(core, whole, core * 256)
    zacc[...] = jnp.zeros_like(zacc)

    pl.semaphore_wait(barrier, 8)
    mine = pl.ds(pl.multiple_of(core * 256, 256), 256)
    swap = pltpu.make_async_remote_copy(
        src_ref=outbox, dst_ref=whole.at[mine], send_sem=swap_sem.at[0], recv_sem=swap_sem.at[1],
        device_id=sib, device_id_type=MESH,
    )
    swap.start()
    swap.wait()

    every = slice(None)

    ahead = [lax.rem(b + k, 4) for k in range(4)]
    devices = {
        "S1p": first_axis(1), "S1m": first_axis(-1), "S1d": first_axis(2),
        "S2p": second_axis(1), "S2m": second_axis(-1),
    }

    def copy(name, p, cols):
        odd = p % 2 if isinstance(p, int) else lax.rem(p, 2)

        def pick(even, other):
            if isinstance(odd, int):
                return other if odd else even
            return jnp.where(odd == 1, other, even)

        place, device = every, sib
        if name in ("S1p", "S1m", "S1d"):
            row, place, device = b, a, devices[name]
        elif name in ("S2p", "S2m"):
            row, device = b, devices[name]
        elif name == "S3":
            row = pick(ahead[3], ahead[1])
            device = (pick(devices["S2p"][0], devices["S2m"][0]), lay)
        else:
            row = ahead[{"D0": 0, "Dp": 1, "D2": 2, "Dm": 3}[name]]
        block = (core, row, place, every, cols)
        return pltpu.make_async_remote_copy(
            src_ref=g.at[block], dst_ref=g.at[block],
            send_sem=send.at[OP[name]], recv_sem=recv.at[OP[name], p],
            device_id=device, device_id_type=MESH,
        )

    def columns(p):
        start = p * WIDE if isinstance(p, int) else pl.multiple_of(p * WIDE, WIDE)
        return pl.ds(start, WIDE)

    def go(p, *names):
        for name in names:
            copy(name, p, columns(p)).start()

    def got(p, *names):
        for name in names:
            copy(name, p, columns(p)).wait_recv()

    def step2(p):
        got(p, "S1p", "S1m", "S1d")
        go(p, "S2p", "S2m", "D0")

    def step3(p):
        got(p, "S2p", "S2m")
        go(p, "S3", "Dp", "Dm")

    def step4(p):
        got(p, "S3")
        go(p, "D2")

    def ready(p):
        got(p, "D0", "Dp", "Dm", "D2")
        for j in range(CB):
            train_copy(p * CB + j).wait()

    xr = x.reshape(32, 2048, 128)
    even_row = lax.rem(lax.broadcasted_iota(jnp.int32, (ROWS, 128), 0), 2) == 0

    def weights(p):
        cols = pl.ds(pl.multiple_of(p * WIDE, WIDE), WIDE)
        blocks = [(0, iy, iz) for iz in range(4) for iy in range(4)] + [(1, iz, iy) for iz in range(4) for iy in range(4)]
        return jnp.concatenate([g[layer, i, j, :, cols] for layer, i, j in blocks], axis=0)

    def product(p, queries, r):
        span = slice(r * ROWS, (r + 1) * ROWS)
        lhs = jnp.concatenate([xr[p * CB + j, span, :] for j in range(CB)], axis=1)
        both = dot(lhs, queries, NT)
        for half in range(2):
            q = half * 128
            zacc[half, span] += jnp.where(even_row, both[:, q:q + 128], both[:, q + 256:q + 384])

    def products(p):
        ready(p)
        queries = weights(p)
        for r in range(2048 // ROWS):
            product(p, queries, r)

    def reduce_copy(step, r):
        src, dst = ((sb1, rb1), (sb2, rb2))[step]
        return pltpu.make_async_remote_copy(
            src_ref=src.at[r], dst_ref=dst.at[r],
            send_sem=rs_send.at[step, r], recv_sem=rs_recv.at[step, r],
            device_id=(x1, x3)[step ^ (r % 2)], device_id_type=MESH,
        )

    mates = (lay1, 3 - lay)

    def target(which, r):
        return part[pl.ds(pl.multiple_of(which * 64, 64), 64), r * 256:(r + 1) * 256]

    def scatter1(r):
        for half in range(2):
            both = zacc[half, pl.ds(r * ROWS, 256, 2), :] + zacc[half, pl.ds(r * ROWS + 1, 256, 2), :]
            part[half * 128:(half + 1) * 128, r * 256:(r + 1) * 256] = both.T
        sb1[r, 0] = target(mates[r % 2], r).astype(BF16)
        sb1[r, 1] = target(lay2, r).astype(BF16)
        reduce_copy(0, r).start()

    def scatter2(r):
        reduce_copy(0, r).wait_recv()
        sb2[r] = (target(mates[1 - r % 2], r) + rb1[r, 1].astype(F32)).astype(BF16)
        reduce_copy(1, r).start()

    def finish(r):
        reduce_copy(1, r).wait_recv()
        cols = slice(r * 256, (r + 1) * 256)
        total = target(lay, r) + rb1[r, 0].astype(F32) + rb2[r].astype(F32)
        out[:, cols] = jnp.where(ids == tids[:, cols], 0.0, total)

    def when(p, top, what):
        pl.when(jnp.logical_and(p >= 0, p < top))(functools.partial(what, p))

    for p in range(PARTS):
        for cb in range(p * CB, (p + 1) * CB):
            g[core, b, a, :, cb * 128:(cb + 1) * 128] = whole[pl.ds(cb, 16, 32), :].astype(BF16)
        go(p, "S1p", "S1m", "S1d")

    @pl.loop(0, PARTS + 8 - 1)
    def _(s):
        when(s, PARTS, step2)
        when(s - 3, PARTS, step3)
        when(s - 6, PARTS, step4)
        when(s - 8, PARTS - 1, products)

    place = lax.broadcasted_iota(jnp.int32, (64, 64), 0) == lax.broadcasted_iota(jnp.int32, (64, 64), 1)
    ids = jnp.sum(jnp.where(place, qids[...].astype(F32), 0.0), axis=1, keepdims=True).astype(jnp.int32)
    last = PARTS - 1
    ready(last)
    queries = weights(last)
    for r in range(4):
        product(last, queries, r)
        scatter1(r)
    for r in range(4):
        scatter2(r)
    for r in range(4):
        finish(r)

    for name in OPS:
        copy(name, 0, every).wait_send()

    for step in range(2):
        for r in range(4):
            reduce_copy(step, r).wait_send()


def body(train_grads, query_grads, basis_out, basis_in, eigenvalues, train_ids, query_ids):
    train = train_grads.reshape(1024, 2, 32, 128).transpose(0, 2, 1, 3)
    query = query_grads.reshape(8, 2, 32, 128).transpose(0, 2, 1, 3)
    vmem = pl.BlockSpec(memory_space=pltpu.VMEM)
    hbm = pl.BlockSpec(memory_space=pl.ANY)
    dma = pltpu.SemaphoreType.DMA
    scores = pl.pallas_call(
        kernel,
        out_shape=jax.ShapeDtypeStruct((64, 1024), F32),
        in_specs=[hbm, vmem, vmem, vmem, vmem, vmem, vmem],
        out_specs=vmem,
        scratch_shapes=[
            pltpu.VMEM((32, 1024, 2, 128), BF16),
            pltpu.VMEM((512, 128), F32),
            pltpu.VMEM((2, 2, 128, 128), F32),
            pltpu.VMEM((512, 128), F32),
            pltpu.VMEM((256, 128), F32),
            pltpu.VMEM((2, 4, 4, 16, 4096), BF16),
            pltpu.VMEM((2, 2048, 128), F32),
            pltpu.VMEM((256, 1024), F32),
            pltpu.VMEM((4, 2, 64, 256), BF16),
            pltpu.VMEM((4, 2, 64, 256), BF16),
            pltpu.VMEM((4, 64, 256), BF16),
            pltpu.VMEM((4, 64, 256), BF16),
            dma((32,)),
            dma((2,)),
            dma((len(OPS),)),
            dma((len(OPS), PARTS)),
            dma((2, 4)),
            dma((2, 4)),
        ],
        compiler_params=pltpu.CompilerParams(
            collective_id=0, has_side_effects=True, vmem_limit_bytes=56 * 2**20
        ),
    )(
        train, query, basis_out, basis_in, eigenvalues,
        train_ids.reshape(1, -1), query_ids.reshape(1, -1),
    )
    return scores.T


def solution(mesh):
    placed = (
        P("rows", "layer", None),
        P("rows", "layer", None),
        P("layer", None, None),
        P("layer", None, None),
        P("layer", None, None),
        P("rows"),
        P("layer"),
    )
    return jax.shard_map(
        body, mesh=mesh, in_specs=placed, out_specs=P("rows", "layer"), check_vma=False
    )
```

time: 123 us -> 44.8 us (0.36)
  waiting for transfers between devices: 71.7 us -> 0 us
  Pallas kernels: 0 us -> 42.7 us
  matrix products: 32.6 us -> 0 us
  between operations: 13.5 us -> 0.01 us
  other arithmetic: 2.62 us -> 0 us
    all_gather x1 -> x0, waiting for transfers between devices: 48.8 us -> none  [body(): piece = lax.all_gather(mine, 'rows', axis=0, tiled=True)]
    pallas_call x0 -> x1, Pallas kernels: none -> 42.7 us  [body(): pl.pallas_call(kernel, out_shape=jax.ShapeDtypeStruct((64, 1024), F32), i...]
    dot_general x5 -> x0, matrix products: 32.6 us -> none  [the longest x1 28.3 us: body(): lax.dot_general(flat_train, flat_piece, (((1,), (1,)), ((), ())), preferr...]
    reduce_scatter x1 -> x0, waiting for transfers between devices: 22.9 us -> none  [body(): raw = lax.psum_scatter(terms, 'layer', scatter_dimension=1, tiled=True)]
    select_n x1 -> x0, other arithmetic: 1.74 us -> none  [body(): return jnp.where(same, jnp.float32(0.0), raw)]
    unnamed x6 -> x1, local copies, waits for them, and re-layouts: 0.02 us -> 1.67 us
  transfers between devices with their start and end apart: 2 -> 0, of which waited for: 2 -> 0; matrix products, arithmetic and copies ran while one was open for 0% -> 0% of each run, Pallas kernels for 0% -> 0%
where the time goes in v2:
time: 44.8 us; the launch traced here: 44.4 us
  Pallas kernels  42.7 us (95%)
  local copies, waits for them, and re-layouts  1.67 us (4%)
    pallas_call x1, Pallas kernels, body(): pl.pallas_call(kernel, out_shape=jax.ShapeDtypeStruct((64, 1024), F32), i...  42.7 us
    unnamed x1, local copies, waits for them, and re-layouts  1.67 us

profile of v2, /device:TPU:0, one launch (start us, length us, event | category | flops | bytes accessed | tf_op | source)
XLA Modules:
  0.0 44.4 jit_solution(16684614669857972040)
XLA Ops:
  0.0 42.7 %shard_map.73 = f32[64,1024]{1,0:T(8,128)} custom-call(bf16[1024,32,2,128]{3,2,1,0:T(2,128)(2,1)} %bitcast.9, bf16[8,32,2,128]{3,2,1,0:T(2,128)(2,1)} %bitcast.11, f32[2,64,64]{2,1,0:T(8,128)} %basis_out.1, f32[2,64,64]{2,1,0:T(8,128)} %basis_in.1, f32[2,64,64]{2,1,0:T(8,128)} %eigenvalues.1, s32[1,1024]{1,0:T(1,128)} %bitcast.12, s32[1,64]{1,0:T(1,128)} %bitcast.13), custom_call_target="tpu_custom_call" | custom-call | tf_op jit(solution)/shard_map/pallas_call | solution.py:297
  42.7 1.7 %copy.9 = f32[1024,64]{0,1:T(8,128)} copy(f32[1024,64]{0,1:T(8,128)} %bitcast.10) | data formatting | bytes 524288

commit v3 on v2

--- a/solution.py
+++ b/solution.py
@@ -47,9 +47,9 @@
 
 
 def kernel(
-    train, query, basis_out, basis_in, eigenvalues, tids, qids, out,
-    x, flat, shaped, whole, outbox, g, zacc, part, sb1, rb1, sb2, rb2,
-    train_sem, swap_sem, send, recv, rs_send, rs_recv,
+    train, query_in, basis_out_in, basis_in_in, eigenvalues_in, tids_in, qids_in, out,
+    query, basis_out, basis_in, eigenvalues, tids, qids, x, flat, shaped, whole, outbox, g, zacc, part, sb1, rb1, sb2, rb2,
+    load_sem, train_sem, swap_sem, send, recv, rs_send, rs_recv,
 ):
     rows, lay = lax.axis_index("rows"), lax.axis_index("layer")
     core = lax.rem(rows, 2)
@@ -76,12 +76,24 @@
     for other in (sib, at(1, 0), at(-1, 0), at(0, 1), at(0, -1), first_axis(2), x1, x3):
         pl.semaphore_signal(barrier, inc=1, device_id=other, device_id_type=MESH)
 
+    loads = [
+        pltpu.make_async_copy(src, dst, load_sem.at[place])
+        for place, (src, dst) in enumerate((
+            (query_in, query), (basis_out_in, basis_out), (basis_in_in, basis_in),
+            (eigenvalues_in, eigenvalues), (tids_in, tids), (qids_in, qids),
+        ))
+    ]
+    for load in loads:
+        load.start()
+
     def train_copy(cb):
         return pltpu.make_async_copy(train.at[:, cb], x.at[cb], train_sem.at[cb])
 
     for cb in range(32):
         train_copy(cb).start()
 
+    for load in loads:
+        load.wait()
     flat[...] = query.reshape(512, 128)[...].astype(F32)
     low = lax.broadcasted_iota(jnp.int32, (32, 128), 1) < 64
     for layer in range(2):
@@ -260,12 +272,12 @@
             g[core, b, a, :, cb * 128:(cb + 1) * 128] = whole[pl.ds(cb, 16, 32), :].astype(BF16)
         go(p, "S1p", "S1m", "S1d")
 
-    @pl.loop(0, PARTS + 8 - 1)
+    @pl.loop(0, PARTS + 7 - 1)
     def _(s):
+        when(s - 7, PARTS - 1, products)
         when(s, PARTS, step2)
         when(s - 3, PARTS, step3)
         when(s - 6, PARTS, step4)
-        when(s - 8, PARTS - 1, products)
 
     place = lax.broadcasted_iota(jnp.int32, (64, 64), 0) == lax.broadcasted_iota(jnp.int32, (64, 64), 1)
     ids = jnp.sum(jnp.where(place, qids[...].astype(F32), 0.0), axis=1, keepdims=True).astype(jnp.int32)
@@ -275,10 +287,14 @@
     for r in range(4):
         product(last, queries, r)
         scatter1(r)
-    for r in range(4):
-        scatter2(r)
-    for r in range(4):
-        finish(r)
+    scatter2(0)
+    scatter2(1)
+    scatter2(2)
+    finish(0)
+    scatter2(3)
+    finish(1)
+    finish(2)
+    finish(3)
 
     for name in OPS:
         copy(name, 0, every).wait_send()
@@ -292,14 +308,20 @@
     train = train_grads.reshape(1024, 2, 32, 128).transpose(0, 2, 1, 3)
     query = query_grads.reshape(8, 2, 32, 128).transpose(0, 2, 1, 3)
     vmem = pl.BlockSpec(memory_space=pltpu.VMEM)
-    hbm = pl.BlockSpec(memory_space=pl.ANY)
+    hbm = pl.BlockSpec(memory_space=pltpu.HBM)
     dma = pltpu.SemaphoreType.DMA
     scores = pl.pallas_call(
         kernel,
         out_shape=jax.ShapeDtypeStruct((64, 1024), F32),
-        in_specs=[hbm, vmem, vmem, vmem, vmem, vmem, vmem],
+        in_specs=[hbm] * 7,
         out_specs=vmem,
         scratch_shapes=[
+            pltpu.VMEM((8, 32, 2, 128), BF16),
+            pltpu.VMEM((2, 64, 64), F32),
+            pltpu.VMEM((2, 64, 64), F32),
+            pltpu.VMEM((2, 64, 64), F32),
+            pltpu.VMEM((1, 1024), jnp.int32),
+            pltpu.VMEM((1, 64), jnp.int32),
             pltpu.VMEM((32, 1024, 2, 128), BF16),
             pltpu.VMEM((512, 128), F32),
             pltpu.VMEM((2, 2, 128, 128), F32),
@@ -312,6 +334,7 @@
             pltpu.VMEM((4, 2, 64, 256), BF16),
             pltpu.VMEM((4, 64, 256), BF16),
             pltpu.VMEM((4, 64, 256), BF16),
+            dma((6,)),
             dma((32,)),
             dma((2,)),
             dma((len(OPS),)),
@@ -320,11 +343,16 @@
             dma((2, 4)),
         ],
         compiler_params=pltpu.CompilerParams(
-            collective_id=0, has_side_effects=True, vmem_limit_bytes=56 * 2**20
+            collective_id=0, has_side_effects=True, vmem_limit_bytes=50 * 2**20
         ),
     )(
-        train, query, basis_out, basis_in, eigenvalues,
-        train_ids.reshape(1, -1), query_ids.reshape(1, -1),
+        *(
+            pltpu.with_memory_space_constraint(value, pltpu.HBM)
+            for value in (
+                train, query, basis_out, basis_in, eigenvalues,
+                train_ids.reshape(1, -1), query_ids.reshape(1, -1),
+            )
+        )
     )
     return scores.T
 

time: 44.8 us -> 56 us (1.25)
  Pallas kernels: 42.7 us -> 55.2 us
  local copies, waits for them, and re-layouts: 1.67 us -> 0.71 us
    pallas_call x1, Pallas kernels: 42.7 us -> 55.2 us  [body(): pl.pallas_call(kernel, out_shape=jax.ShapeDtypeStruct((64, 1024), F32), i...]
    unnamed x1, local copies, waits for them, and re-layouts: 1.67 us -> 0.71 us
where the time goes in v3:
time: 56 us; the launch traced here: 55.9 us
  Pallas kernels  55.2 us (99%)
  local copies, waits for them, and re-layouts  0.71 us (1%)
    pallas_call x1, Pallas kernels, body(): pl.pallas_call(kernel, out_shape=jax.ShapeDtypeStruct((64, 1024), F32), i...  55.2 us

profile of v3, /device:TPU:0, one launch (start us, length us, event | category | flops | bytes accessed | tf_op | source)
XLA Modules:
  0.0 55.9 jit_solution(12363512501663218240)
XLA Ops:
  0.0 55.2 %shard_map.73 = f32[64,1024]{1,0:T(8,128)S(1)} custom-call(bf16[1024,32,2,128]{3,2,1,0:T(2,128)(2,1)} %bitcast.10, bf16[8,32,2,128]{3,2,1,0:T(2,128)(2,1)} %bitcast.11, f32[2,64,64]{2,1,0:T(8,128)} %basis_out_in.1, f32[2,64,64]{2,1,0:T(8,128)} %basis_in_in.1, f32[2,64,64]{2,1,0:T(8,128)} %eigenvalues_in.1, s32[1,1024]{1,0:T(1,128)} %bitcast.12, s32[1,64]{1,0:T(1,128)} %bitcast.13), custom_call_target="tpu_custom_call" | custom-call | tf_op jit(solution)/shard_map/pallas_call | solution.py:313
  55.2 0.7 %copy.9 = f32[1024,64]{0,1:T(8,128)} copy(f32[1024,64]{0,1:T(8,128)S(1)} %bitcast.9) | data formatting | bytes 524288

commit v4 on v3

--- a/solution.py
+++ b/solution.py
@@ -274,10 +274,10 @@
 
     @pl.loop(0, PARTS + 7 - 1)
     def _(s):
-        when(s - 7, PARTS - 1, products)
         when(s, PARTS, step2)
         when(s - 3, PARTS, step3)
         when(s - 6, PARTS, step4)
+        when(s - 7, PARTS - 1, products)
 
     place = lax.broadcasted_iota(jnp.int32, (64, 64), 0) == lax.broadcasted_iota(jnp.int32, (64, 64), 1)
     ids = jnp.sum(jnp.where(place, qids[...].astype(F32), 0.0), axis=1, keepdims=True).astype(jnp.int32)

time: 56 us -> 48.2 us (0.86)
  Pallas kernels: 55.2 us -> 47.4 us
    pallas_call x1, Pallas kernels: 55.2 us -> 47.4 us  [body(): pl.pallas_call(kernel, out_shape=jax.ShapeDtypeStruct((64, 1024), F32), i...]
where the time goes in v4:
time: 48.2 us; the launch traced here: 48.1 us
  Pallas kernels  47.4 us (98%)
  local copies, waits for them, and re-layouts  0.71 us (1%)
    pallas_call x1, Pallas kernels, body(): pl.pallas_call(kernel, out_shape=jax.ShapeDtypeStruct((64, 1024), F32), i...  47.4 us

profile of v4, /device:TPU:0, one launch (start us, length us, event | category | flops | bytes accessed | tf_op | source)
XLA Modules:
  0.0 48.1 jit_solution(7154702114314519825)
XLA Ops:
  0.0 47.4 %shard_map.73 = f32[64,1024]{1,0:T(8,128)S(1)} custom-call(bf16[1024,32,2,128]{3,2,1,0:T(2,128)(2,1)} %bitcast.10, bf16[8,32,2,128]{3,2,1,0:T(2,128)(2,1)} %bitcast.11, f32[2,64,64]{2,1,0:T(8,128)} %basis_out_in.1, f32[2,64,64]{2,1,0:T(8,128)} %basis_in_in.1, f32[2,64,64]{2,1,0:T(8,128)} %eigenvalues_in.1, s32[1,1024]{1,0:T(1,128)} %bitcast.12, s32[1,64]{1,0:T(1,128)} %bitcast.13), custom_call_target="tpu_custom_call" | custom-call | tf_op jit(solution)/shard_map/pallas_call | solution.py:313
  47.4 0.7 %copy.9 = f32[1024,64]{0,1:T(8,128)} copy(f32[1024,64]{0,1:T(8,128)S(1)} %bitcast.9) | data formatting | bytes 524288

commit v5 on v4

--- a/solution.py
+++ b/solution.py
@@ -89,11 +89,11 @@
     def train_copy(cb):
         return pltpu.make_async_copy(train.at[:, cb], x.at[cb], train_sem.at[cb])
 
+    for load in loads:
+        load.wait()
     for cb in range(32):
         train_copy(cb).start()
 
-    for load in loads:
-        load.wait()
     flat[...] = query.reshape(512, 128)[...].astype(F32)
     low = lax.broadcasted_iota(jnp.int32, (32, 128), 1) < 64
     for layer in range(2):
@@ -287,14 +287,10 @@
     for r in range(4):
         product(last, queries, r)
         scatter1(r)
-    scatter2(0)
-    scatter2(1)
-    scatter2(2)
-    finish(0)
-    scatter2(3)
-    finish(1)
-    finish(2)
-    finish(3)
+    for r in range(4):
+        scatter2(r)
+    for r in range(4):
+        finish(r)
 
     for name in OPS:
         copy(name, 0, every).wait_send()

time: 48.2 us -> 42.1 us (0.87)
  Pallas kernels: 47.4 us -> 41 us
    pallas_call x1, Pallas kernels: 47.4 us -> 41 us  [body(): pl.pallas_call(kernel, out_shape=jax.ShapeDtypeStruct((64, 1024), F32), i...]
where the time goes in v5:
time: 42.1 us; the launch traced here: 41.7 us
  Pallas kernels  41 us (97%)
  local copies, waits for them, and re-layouts  0.71 us (2%)
    pallas_call x1, Pallas kernels, body(): pl.pallas_call(kernel, out_shape=jax.ShapeDtypeStruct((64, 1024), F32), i...  41 us

profile of v5, /device:TPU:0, one launch (start us, length us, event | category | flops | bytes accessed | tf_op | source)
XLA Modules:
  0.0 41.7 jit_solution(847704607058799709)
XLA Ops:
  0.0 41.0 %shard_map.73 = f32[64,1024]{1,0:T(8,128)S(1)} custom-call(bf16[1024,32,2,128]{3,2,1,0:T(2,128)(2,1)} %bitcast.10, bf16[8,32,2,128]{3,2,1,0:T(2,128)(2,1)} %bitcast.11, f32[2,64,64]{2,1,0:T(8,128)} %basis_out_in.1, f32[2,64,64]{2,1,0:T(8,128)} %basis_in_in.1, f32[2,64,64]{2,1,0:T(8,128)} %eigenvalues_in.1, s32[1,1024]{1,0:T(1,128)} %bitcast.12, s32[1,64]{1,0:T(1,128)} %bitcast.13), custom_call_target="tpu_custom_call" | custom-call | tf_op jit(solution)/shard_map/pallas_call | solution.py:309
  41.0 0.7 %copy.9 = f32[1024,64]{0,1:T(8,128)} copy(f32[1024,64]{0,1:T(8,128)S(1)} %bitcast.9) | data formatting | bytes 524288

commit v6 on v5

--- a/solution.py
+++ b/solution.py
@@ -272,12 +272,12 @@
             g[core, b, a, :, cb * 128:(cb + 1) * 128] = whole[pl.ds(cb, 16, 32), :].astype(BF16)
         go(p, "S1p", "S1m", "S1d")
 
-    @pl.loop(0, PARTS + 7 - 1)
+    @pl.loop(0, PARTS + 8 - 1)
     def _(s):
         when(s, PARTS, step2)
-        when(s - 3, PARTS, step3)
-        when(s - 6, PARTS, step4)
-        when(s - 7, PARTS - 1, products)
+        when(s - 4, PARTS, step3)
+        when(s - 7, PARTS, step4)
+        when(s - 8, PARTS - 1, products)
 
     place = lax.broadcasted_iota(jnp.int32, (64, 64), 0) == lax.broadcasted_iota(jnp.int32, (64, 64), 1)
     ids = jnp.sum(jnp.where(place, qids[...].astype(F32), 0.0), axis=1, keepdims=True).astype(jnp.int32)

time: 42.1 us -> 42.5 us (level)
    pallas_call x1, Pallas kernels: 41 us -> 41.4 us  [body(): pl.pallas_call(kernel, out_shape=jax.ShapeDtypeStruct((64, 1024), F32), i...]
where the time goes in v6:
time: 42.5 us; the launch traced here: 42.1 us
  Pallas kernels  41.4 us (97%)
  local copies, waits for them, and re-layouts  0.71 us (2%)
    pallas_call x1, Pallas kernels, body(): pl.pallas_call(kernel, out_shape=jax.ShapeDtypeStruct((64, 1024), F32), i...  41.4 us

profile of v6, /device:TPU:0, one launch (start us, length us, event | category | flops | bytes accessed | tf_op | source)
XLA Modules:
  0.0 42.1 jit_solution(13259865675880803868)
XLA Ops:
  0.0 41.4 %shard_map.73 = f32[64,1024]{1,0:T(8,128)S(1)} custom-call(bf16[1024,32,2,128]{3,2,1,0:T(2,128)(2,1)} %bitcast.10, bf16[8,32,2,128]{3,2,1,0:T(2,128)(2,1)} %bitcast.11, f32[2,64,64]{2,1,0:T(8,128)} %basis_out_in.1, f32[2,64,64]{2,1,0:T(8,128)} %basis_in_in.1, f32[2,64,64]{2,1,0:T(8,128)} %eigenvalues_in.1, s32[1,1024]{1,0:T(1,128)} %bitcast.12, s32[1,64]{1,0:T(1,128)} %bitcast.13), custom_call_target="tpu_custom_call" | custom-call | tf_op jit(solution)/shard_map/pallas_call | solution.py:309
  41.4 0.7 %copy.9 = f32[1024,64]{0,1:T(8,128)} copy(f32[1024,64]{0,1:T(8,128)S(1)} %bitcast.9) | data formatting | bytes 524288
